TPU v7x, 32 devices: a whole 2x2x4 slice. The times are simulated.
32 devices in a mesh: section: 4 (over y, x), row: 4 (over z), col: 2 (over core).
Axes of the slice: x: 2, y: 2, z: 4, core: 2. Of those that a mesh axis runs over, the one named last changes fastest.
Arguments:
- statistic: float32 [8192, 2048], P(('section', 'row'), 'col'), parts along dimension 0, as said below
- gradient: bfloat16 [8192, 28672], P('section', ('row', 'col')), parts along dimension 0, may hold values from -6 to 6
Outputs:
- next_m: float32 [8192, 2048], P(('section', 'row'), 'col'), parts along dimension 0
- preconditioned: bfloat16 [8192, 28672], P('section', ('row', 'col')), parts along dimension 0
- next_diag: float32 [8192], P(('section', 'row')), parts along dimension 0
There are 4 independent parts, one for each index of `section`. A program takes and returns all parts, laid end to end along the dimension named above; each array names one. Nothing has to cross between parts.
Inputs may be any that keep to these rules, and one draw needn't show every extreme that they name: `statistic`: symmetric and positive definite.
All inputs are finite; a program needn't handle non-finite values.
Results may differ from a plain program's by a relative error of at most 0.0052.
Values may be sent and summed in bfloat16 or wider, within the bound.
A program may use at most 128 MiB of HBM per device.

v0:
```python
import jax
import jax.numpy as jnp
from jax import lax
from jax.sharding import PartitionSpec as P

BLOCK = 2048


def fold_with(panel, piece):
    return jnp.dot(
        panel, piece, precision=lax.Precision.HIGHEST, preferred_element_type=jnp.float32
    )


def local(statistic, gradient):
    highest = lax.Precision.HIGHEST
    rows_here, cols_here = statistic.shape
    total = lax.psum(jnp.sum(statistic * statistic), ("row", "col"))
    scale4 = jnp.sqrt(BLOCK * (total / (BLOCK * BLOCK) + 1e-06))
    row_ids = lax.axis_index("row") * rows_here + jnp.arange(rows_here, dtype=jnp.int32)
    col_start = lax.axis_index("col") * cols_here
    col_ids = col_start + jnp.arange(cols_here, dtype=jnp.int32)
    ident = (row_ids[:, None] == col_ids[None, :]).astype(jnp.float32)
    m_start = statistic / scale4
    t_block = (5.0 * ident - m_start) / 4.0
    t_rows = lax.all_gather(t_block, "col", axis=1, tiled=True)
    m_cols = lax.all_gather(m_start, "row", axis=0, tiled=True)
    every_row = jnp.arange(BLOCK, dtype=jnp.int32)
    ident_cols = (every_row[:, None] == col_ids[None, :]).astype(jnp.float32)
    t_cols = (5.0 * ident_cols - m_cols) / 4.0
    square = jnp.dot(t_rows, t_cols, precision=highest, preferred_element_type=jnp.float32)
    square_rows = lax.all_gather(square, "col", axis=1, tiled=True)
    third = jnp.dot(square_rows, m_cols, precision=highest, preferred_element_type=jnp.float32)
    full_block = fold_with(square_rows, lax.all_gather(third, "row", axis=0, tiled=True))
    next_m = full_block * (1.0 - ident)
    square_own = lax.dynamic_slice_in_dim(square_rows, col_start, cols_here, 1)
    partial_diag = jnp.sum(square_own * third, axis=1)
    next_diag = lax.psum(partial_diag, "col")
    fourth_root = jnp.sqrt(jnp.sqrt(scale4))
    x_block = (t_block / fourth_root).astype(jnp.bfloat16)
    spread = lax.all_gather(x_block, ("row", "col"), axis=1, tiled=True)
    grid_rows = lax.axis_size("row")
    grid_cols = lax.axis_size("col")
    arranged = spread.reshape(rows_here, grid_rows, grid_cols, cols_here)
    grad_split = gradient.reshape(grid_cols, cols_here, gradient.shape[1])
    product = jnp.einsum("aijc,jcf->iaf", arranged, grad_split, preferred_element_type=jnp.float32)
    preconditioned = product.reshape(BLOCK, gradient.shape[1]).astype(jnp.bfloat16)
    return (next_m, preconditioned, next_diag)


def solution(mesh):
    return jax.shard_map(
        local,
        mesh=mesh,
        in_specs=(P(("section", "row"), "col"), P("section", ("row", "col"))),
        out_specs=(
            P(("section", "row"), "col"),
            P("section", ("row", "col")),
            P(("section", "row")),
        ),
        check_vma=False,
    )
```

profile of v0, /device:TPU:0, one launch (start us, length us, event | category | flops | bytes accessed | tf_op | source)
XLA Modules:
  0.0 488.5 jit_solution(13225213153502750366)
XLA Ops:
  7.2 0.0 all-gather.6.cloned.1.call-start
  7.2 2.7 multiply_reduce_fusion.1
  10.0 18.7 %psum.14 = f32[]{:T(128)} all-reduce(f32[]{:T(128)} %multiply_reduce_fusion.1), channel_id=1, replica_groups=mesh['section'=4,'row'=4,'col'=2] {'row','col'}, use_global_device_ids=true, to_apply=%region_1.0 | all-reduce | flops 1 | bytes 8 | tf_op jit(solution)/shard_map/psum | solution.py:18
  29.4 4.5 divide_convert_fusion
  33.9 0.0 all-gather.6.cloned.1.call-update
  33.9 0.0 all-gather.8.cloned.1.call-start
  34.0 0.7 all-gather.8.cloned.1.call-update
  34.7 0.0 all-gather.10.cloned.1.call-start
  34.7 11.2 %all-gather.6.cloned.1.call-done = f32[512,2048]{1,0:T(8,128)} async-done(((f32[512,1024]{1,0:T(8,128)}), f32[512,2048]{1,0:T(8,128)}) %all-gather.6.cloned.1.call-update) | async-done | bytes 4194320 | tf_op jit(solution)/shard_map/all_gather | solution.py:26
  46.0 153.0 %all-gather.8.cloned.1.call-done = f32[2048,1024]{1,0:T(8,128)} async-done(((f32[512,1024]{1,0:T(8,128)}), f32[2048,1024]{1,0:T(8,128)}) %all-gather.8.cloned.1.call-update) | async-done | bytes 8388624 | tf_op jit(solution)/shard_map/all_gather | solution.py:27
  199.0 18.1 %fusion.1 = f32[512,1024]{1,0:T(8,128)} fusion(f32[512,2048]{1,0:T(8,128)} %all-gather.6.cloned.1.call-done, f32[2048,1024]{1,0:T(8,128)} %all-gather.8.cloned.1.call-done, s32[1024]{0:T(1024)S(1)} %iota_add_fusion), kind=kOutput, calls=%fused_computation.2 | convolution fusion | flops 12893290496 | bytes 14684160 | tf_op jit(solution)/shard_map/dot_general | solution.py:31
  217.1 0.0 all-gather.10.cloned.1.call-update
  217.1 0.0 all-gather.14.cloned.1.call-start
  217.1 0.5 all-gather.14.cloned.1.call-update
  217.7 0.0 all-gather.12.cloned.1.call-start
  217.7 11.4 %all-gather.10.cloned.1.call-done = f32[512,2048]{1,0:T(8,128)} async-done(((f32[512,1024]{1,0:T(8,128)}), f32[512,2048]{1,0:T(8,128)}) %all-gather.10.cloned.1.call-update) | async-done | bytes 4194320 | tf_op jit(solution)/shard_map/all_gather | solution.py:32
  229.1 18.5 %multiply_reduce_fusion = (f32[512]{0:T(512)S(1)}, f32[512,1024]{1,0:T(8,128)}) fusion(f32[512,2048]{1,0:T(8,128)} %all-gather.10.cloned.1.call-done, s32[]{:T(128)S(6)} %select_n.3, f32[2048,1024]{1,0:T(8,128)} %all-gather.8.cloned.1.call-done), kind=kOutput, calls=%fused_computation.17 | convolution fusion | flops 12885950464 | bytes 16779268 | tf_op jit(solution)/shard_map/dot_general | solution.py:33
  247.7 0.0 all-gather.12.cloned.1.call-update
  247.7 66.2 %all-gather.14.cloned.1.call-done = bf16[512,8192]{1,0:T(8,128)(2,1)} async-done(((bf16[512,1024]{1,0:T(8,128)(2,1)}), bf16[512,8192]{1,0:T(8,128)(2,1)}) %all-gather.14.cloned.1.call-update) | async-done | bytes 8388624 | tf_op jit(solution)/shard_map/all_gather | solution.py:41
  313.9 14.8 %reshape.22 = bf16[512,4,2,1024]{3,2,1,0:T(2,128)(2,1)} reshape(bf16[512,8192]{1,0:T(8,128)(2,1)} %all-gather.14.cloned.1.call-done) | data formatting | bytes 16777216 | tf_op jit(solution)/shard_map/reshape | solution.py:44
  328.7 82.3 %bitcast_convert_fusion = bf16[512,4,3584]{2,0,1:T(8,128)(2,1)} fusion(bf16[2,1024,3584,1]{2,1,0,3:T(8,128)(2,1)} %bitcast.15, bf16[512,4,2,1024]{3,2,1,0:T(2,128)(2,1)} %reshape.22), kind=kOutput, calls=%fused_computation | convolution fusion | flops 30072111104 | bytes 37748736 | tf_op jit(solution)/shard_map/aijc,jcf->iaf/dot_general | solution.py:46
  411.0 3.0 psum.15
  414.0 50.0 %all-gather.12.cloned.1.call-done = f32[2048,1024]{1,0:T(8,128)} async-done(((f32[512,1024]{1,0:T(8,128)}), f32[2048,1024]{1,0:T(8,128)}) %all-gather.12.cloned.1.call-update) | async-done | bytes 8388624 | tf_op jit(solution)/shard_map/all_gather | solution.py:34
  464.1 17.9 %fusion.12 = f32[512,1024]{1,0:T(8,128)} fusion(f32[512,2048]{1,0:T(8,128)} %all-gather.10.cloned.1.call-done, f32[2048,1024]{1,0:T(8,128)} %all-gather.12.cloned.1.call-done, s32[1024]{0:T(1024)S(1)} %iota_add_fusion, s32[512]{0:T(512)S(1)} %iota_add_fusion.1), kind=kOutput, calls=%fused_computation.16 | convolution fusion | flops 12886999040 | bytes 14686208 | tf_op jit(solution)/shard_map/dot_general | solution.py:10
  (2 shorter events, 0.0 us)
Async XLA Ops:
  7.2 38.8 %all-gather.6.cloned.1.call-start = ((), (), s32[]{:S(2)}) async-start(), calls=%async_computation | async-start | bytes 6291456 | tf_op jit(solution)/shard_map/all_gather | solution.py:26
  33.9 165.0 %all-gather.8.cloned.1.call-start = ((), (), s32[]{:S(2)}) async-start(), calls=%async_computation.1 | async-start | bytes 10485760 | tf_op jit(solution)/shard_map/all_gather | solution.py:27
  34.7 194.5 %all-gather.10.cloned.1.call-start = ((), (), s32[]{:S(2)}) async-start(), calls=%async_computation.2 | async-start | bytes 6291456 | tf_op jit(solution)/shard_map/all_gather | solution.py:32
  217.1 96.8 %all-gather.14.cloned.1.call-start = ((), (), s32[]{:S(2)}) async-start(), calls=%async_computation.4 | async-start | bytes 9437184 | tf_op jit(solution)/shard_map/all_gather | solution.py:41
  217.7 246.4 %all-gather.12.cloned.1.call-start = ((), (), s32[]{:S(2)}) async-start(), calls=%async_computation.3 | async-start | bytes 10485760 | tf_op jit(solution)/shard_map/all_gather | solution.py:34
Sparse Core Ops, SparseCore 0:
  34.1 11.8 all-gather.5
  48.1 150.7 all-gather.7
  217.2 11.8 all-gather.9
  230.6 83.2 all-gather.13
  315.9 148.1 all-gather.11
where the time goes:
time: 489 us; the launch traced here: 488 us
  waiting for transfers between devices  293 us (60%)
  matrix products  137 us (28%)
  blocking collectives  21.7 us (4%)
  local copies, waits for them, and re-layouts  14.8 us (3%)
  between operations  14.6 us (3%)
  other arithmetic  7.21 us (1%)
    all_gather x1, waiting for transfers between devices, local(): m_cols = lax.all_gather(m_start, 'row', axis=0, tiled=True)  153 us
    dot_general x1, matrix products, local(): jnp.einsum('aijc,jcf->iaf', arranged, grad_split, preferred_element_type=...  82.3 us
    all_gather x1, waiting for transfers between devices, local(): spread = lax.all_gather(x_block, ('row', 'col'), axis=1, tiled=True)  66.2 us
    all_gather x1, waiting for transfers between devices, local(): lax.all_gather(third, 'row', axis=0, tiled=True)  50 us
    psum x1, blocking collectives, local(): total = lax.psum(jnp.sum(statistic * statistic), ('row', 'col'))  18.7 us
    dot_general x1, matrix products, local(): jnp.dot(square_rows, m_cols, precision=highest, preferred_element_type=jn...  18.5 us
    dot_general x1, matrix products, local(): jnp.dot(t_rows, t_cols, precision=highest, preferred_element_type=jnp.flo...  18.1 us
    dot_general x1, matrix products, fold_with(): jnp.dot(panel, piece, precision=lax.Precision.HIGHEST, preferred_element_...  17.9 us
  transfers between devices with their start and end apart: 5, of which 5 were waited for; matrix products, arithmetic and copies ran while one was open for 24% of the time, Pallas kernels for 0%

commit v1 on v0

v1 whole, which is shorter than its diff:
```python
import functools

import jax
import jax.numpy as jnp
from jax import lax
from jax.experimental import pallas as pl
from jax.experimental.pallas import tpu as pltpu
from jax.sharding import PartitionSpec as P

F32, BF16 = jnp.float32, jnp.bfloat16
MIB = 1024 * 1024


def split(extent, most):
    step = most
    while extent % step:
        step -= 128
    return step


def coefficients(total, n):
    scale4 = jnp.sqrt(n * (total / (n * n) + 1e-06))
    return scale4, jnp.sqrt(jnp.sqrt(scale4))


def exchange_kernel(
    R, C, s_ref, g_ref, y_ref, sf_out, info_out,
    sf, gv, yv, mine, notes,
    g_sem, y_sem, o_sem, send_sem, fwd_sem, recv_sem, note_send, note_recv,
):
    z, c = lax.axis_index("row"), lax.axis_index("col")
    bs, width = s_ref.shape
    n = sf.shape[0]
    nf = gv.shape[1]
    H = R // C
    sib = 1 - c

    def block(ref, a, b):
        return ref.at[
            pl.ds(pl.multiple_of(a * bs, bs), bs), pl.ds(pl.multiple_of(b * bs, bs), bs)
        ]

    def chosen(s, o, t):
        ds, do = jnp.abs(s - t), jnp.abs(o - t)
        low = jnp.where(t < R // 2, 1, 0)
        tie = jnp.where(low == 1, jnp.where(s < o, 1, 0), jnp.where(s > o, 1, 0))
        pick = jnp.where(ds < do, 1, jnp.where(ds == do, tie, 0))
        return jnp.where(s == o, 1, pick)

    def sends(p, act):
        def body(idx, carry):
            h, side = idx // 2, idx % 2
            t = z + p * (2 * side - 1)
            b = c * H + h
            ok = (t >= 0) & (t < R) & (t != b)

            @pl.when(ok & (chosen(z, b, t) == 1))
            def _():
                act(
                    pltpu.make_async_remote_copy(
                        src_ref=block(sf, z, b), dst_ref=block(sf, z, b),
                        send_sem=send_sem.at[p, h, side], recv_sem=recv_sem.at[z, b],
                        device_id={"row": t, "col": c},
                        device_id_type=pl.DeviceIdType.MESH,
                    )
                )
            return carry
        lax.fori_loop(0, 2 * H, body, 0)

    def to_sibling(a, b):
        return pltpu.make_async_remote_copy(
            src_ref=block(sf, a, b), dst_ref=block(sf, a, b),
            send_sem=fwd_sem.at[a, b], recv_sem=recv_sem.at[a, b],
            device_id={"col": sib}, device_id_type=pl.DeviceIdType.MESH,
        )

    def mirror(s, o):
        @pl.when(s != o)
        def _():
            block(sf, o, s)[...] = block(sf, s, o)[...].T

    def arrivals(p):
        for direct in (True, False):
            def body(idx, carry):
                side, h = idx // H, idx % H
                s = z + p * (2 * side - 1)
                o = (c if direct else sib) * H + h
                ok = (s >= 0) & (s < R) & (o != z)

                @pl.when(ok & (chosen(s, o, z) == 1))
                def _():
                    to_sibling(s, o).wait_recv()
                    if direct:
                        to_sibling(s, o).start()
                    mirror(s, o)
                return carry
            lax.fori_loop(0, 2 * H, body, 0)

    def forwards_done(p):
        def body(idx, carry):
            side, h = idx // H, idx % H
            s = z + p * (2 * side - 1)
            o = c * H + h
            ok = (s >= 0) & (s < R) & (o != z)

            @pl.when(ok & (chosen(s, o, z) == 1))
            def _():
                to_sibling(s, o).wait_send()
            return carry
        lax.fori_loop(0, 2 * H, body, 0)

    def g_copy(k):
        rows = pl.ds(k * bs, bs)
        return pltpu.make_async_copy(g_ref.at[rows], gv.at[rows], g_sem.at[k])

    for k in range(R):
        g_copy(k).start()

    barrier = pltpu.get_barrier_semaphore()
    for dz in range(R):
        for dc in range(C):
            if dz or dc:
                pl.semaphore_signal(
                    barrier, inc=1,
                    device_id={"row": lax.rem(z + dz, R), "col": lax.rem(c + dc, C)},
                    device_id_type=pl.DeviceIdType.MESH,
                )

    rows_z = pl.ds(pl.multiple_of(z * bs, bs), bs)
    for h in range(H):
        block(sf, z, c * H + h)[...] = s_ref[:, h * bs:(h + 1) * bs].astype(BF16)
    pl.semaphore_wait(barrier, R * C - 1)
    for h in range(H):
        to_sibling(z, c * H + h).start()
    sends(1, lambda d: d.start())

    step = min(bs, 64)

    def scan(r, carry):
        acc, low = carry
        at = pl.multiple_of(r * step, step)
        s = s_ref[pl.ds(at, step), :]
        acc = acc + jnp.sum((s * s).reshape(step // 8, 8, width), axis=0)
        ri = lax.broadcasted_iota(jnp.int32, (step, width), 0) + (z * bs + at)
        ci = lax.broadcasted_iota(jnp.int32, (step, width), 1) + c * width
        left = jnp.where(ri == ci, s - s.astype(BF16).astype(F32), 0.0)
        low = low + jnp.sum(left.reshape(step // 8, 8, width), axis=0)
        return acc, low

    zero = jnp.zeros((8, width), F32)
    acc, low = lax.fori_loop(0, bs // step, scan, (zero, zero))
    mine[:, pl.ds(0, width)] = jnp.sum(low, axis=0, keepdims=True)
    own_total = jnp.sum(jnp.sum(acc, axis=0, keepdims=True), axis=1, keepdims=True)
    mine[:, pl.ds(width, 128)] = jnp.broadcast_to(own_total, (1, 128))

    def note_copy(dz, dc):
        return pltpu.make_async_remote_copy(
            src_ref=mine, dst_ref=notes.at[dz, dc],
            send_sem=note_send.at[dz, dc], recv_sem=note_recv.at[dz, dc],
            device_id={"row": lax.rem(z + dz, R), "col": lax.rem(c + dc, C)},
            device_id_type=pl.DeviceIdType.MESH,
        )

    others = [(dz, dc) for dz in range(R) for dc in range(C) if dz or dc]
    for dz, dc in others:
        note_copy(dz, dc).start()
    notes[0, 0] = mine[...]

    for h in range(H):
        to_sibling(z, sib * H + h).wait_recv()

    def own_mirror(o, carry):
        mirror(z, o)
        return carry
    lax.fori_loop(0, R, own_mirror, 0)

    for k in range(R):
        g_copy(k).wait()
    for dz, dc in others:
        note_copy(dz, dc).wait_recv()
    near = functools.reduce(lambda a, b: a + b, [notes[d, 0] for d in range(R)])
    far = functools.reduce(lambda a, b: a + b, [notes[d, 1] for d in range(R)])
    total = near[:, width:] + far[:, width:]
    info_out[:, pl.ds(pl.multiple_of(c * width, 128), width)] = near[:, :width]
    info_out[:, pl.ds(pl.multiple_of(sib * width, 128), width)] = far[:, :width]
    info_out[:, pl.ds(n, 128)] = total
    scale4, root = coefficients(total[:, :1], n)
    keep, take = 1.25 / root, (0.25 / scale4) / root
    chunk = split(nf, 512)

    def y_copy(i):
        rows = pl.ds(pl.multiple_of(i * bs, bs), bs)
        return pltpu.make_async_copy(yv.at[rows], y_ref.at[rows], y_sem.at[i])

    def compute(i):
        rows = pl.ds(pl.multiple_of(i * bs, bs), bs)

        def body(j, carry):
            cols = pl.ds(pl.multiple_of(j * chunk, chunk), chunk)
            prod = jnp.dot(sf[rows, :], gv[:, cols], preferred_element_type=F32)
            yv[rows, cols] = (keep * gv[rows, cols].astype(F32) - take * prod).astype(BF16)
            return carry
        lax.fori_loop(0, nf // chunk, body, 0)
        y_copy(i).start()

    compute(z)
    for p in range(1, R):
        arrivals(p)
        sends(p, lambda d: d.wait_send())
        if p + 1 < R:
            sends(p + 1, lambda d: d.start())
        else:
            whole = pltpu.make_async_copy(sf, sf_out, o_sem)
            whole.start()

        def both(side, carry):
            i = z + p * (2 * side - 1)

            @pl.when((i >= 0) & (i < R))
            def _():
                compute(i)
            return carry
        lax.fori_loop(0, 2, both, 0)

    for h in range(H):
        to_sibling(z, c * H + h).wait_send()
    for p in range(1, R):
        forwards_done(p)
    for dz, dc in others:
        note_copy(dz, dc).wait_send()
    for i in range(R):
        y_copy(i).wait()
    whole.wait()


def newton_kernel(
    R, C, y_ref, sf, s_ref, info_ref, pre_ref, next_ref, diag_ref,
    held, narrow, y_sem,
):
    z, c = lax.axis_index("row"), lax.axis_index("col")
    bs, width = s_ref.shape
    n = sf.shape[0]

    def y_copy(i):
        rows = pl.ds(i * bs, bs)
        return pltpu.make_async_copy(y_ref.at[rows], pre_ref.at[rows], y_sem.at[i])

    for i in range(R):
        y_copy(i).start()

    scale4, _ = coefficients(info_ref[:, pl.ds(n, 1)], n)
    inv = 1.0 / scale4
    chunk = split(width, 512)
    rows_z = pl.ds(pl.multiple_of(z * bs, bs), bs)

    def ident(at, size):
        ri = lax.broadcasted_iota(jnp.int32, (bs, size), 0) + z * bs
        ci = lax.broadcasted_iota(jnp.int32, (bs, size), 1) + at
        return ri == ci

    def first(j, carry):
        at = pl.multiple_of(j * chunk, chunk)
        cols = pl.ds(at, chunk)
        m = sf[rows_z, cols].astype(F32)
        m = (m + jnp.where(ident(at, chunk), info_ref[:, cols], 0.0)) * inv
        held[0, :, cols] = m
        narrow[0, :, cols] = m.astype(BF16)
        return carry
    lax.fori_loop(0, n // chunk, first, 0)

    def product(now, at):
        cols = pl.ds(at, chunk)
        prod = jnp.dot(narrow[now], sf[:, cols], preferred_element_type=F32)
        r = held[now, :, cols]
        return 1.25 * r - (0.25 * inv) * (prod + r * info_ref[:, cols])

    def turn(step, carry):
        now, later = step % 2, (step + 1) % 2

        def body(j, inner):
            at = pl.multiple_of(j * chunk, chunk)
            r = product(now, at)
            held[later, :, pl.ds(at, chunk)] = r
            narrow[later, :, pl.ds(at, chunk)] = r.astype(BF16)
            return inner
        lax.fori_loop(0, n // chunk, body, 0)
        return carry
    lax.fori_loop(0, 3, turn, 0)

    def last(j, carry):
        at = pl.multiple_of(c * width + j * chunk, chunk)
        r = product(1, at)
        next_ref[:, pl.ds(pl.multiple_of(j * chunk, chunk), chunk)] = jnp.where(
            ident(at, chunk), 0.0, r
        )
        return carry
    lax.fori_loop(0, width // chunk, last, 0)

    def diagonal(j, carry):
        at = pl.multiple_of(j * chunk, chunk)
        cols = pl.ds(at, chunk)
        r = held[1, :, cols]
        on = ident(at, chunk)
        s = sf[rows_z, cols].astype(F32) + jnp.where(on, info_ref[:, cols], 0.0)
        term = jnp.where(on, 1.25 * r, 0.0) - (0.25 * inv) * (r * s)
        return carry + jnp.sum(term, axis=1, keepdims=True)
    diag_ref[...] = lax.fori_loop(0, n // chunk, diagonal, jnp.zeros((bs, 1), F32))

    for i in range(R):
        y_copy(i).wait()


def local_kernels(R, C, statistic, gradient):
    bs, width = statistic.shape
    n, nf = gradient.shape
    vmem, hbm = pl.BlockSpec(memory_space=pltpu.VMEM), pl.BlockSpec(memory_space=pl.ANY)
    dma = pltpu.SemaphoreType.DMA
    H = R // C
    y, sf, info = pl.pallas_call(
        functools.partial(exchange_kernel, R, C),
        out_shape=(
            jax.ShapeDtypeStruct((n, nf), BF16),
            jax.ShapeDtypeStruct((n, n), BF16),
            jax.ShapeDtypeStruct((1, n + 128), F32),
        ),
        in_specs=[vmem, hbm],
        out_specs=(hbm, hbm, vmem),
        scratch_shapes=[
            pltpu.VMEM((n, n), BF16),
            pltpu.VMEM((n, nf), BF16),
            pltpu.VMEM((n, nf), BF16),
            pltpu.VMEM((1, width + 128), F32),
            pltpu.VMEM((R, C, 1, width + 128), F32),
            dma((R,)), dma((R,)), dma,
            dma((R, H, 2)), dma((R, R)), dma((R, R)),
            dma((R, C)), dma((R, C)),
        ],
        compiler_params=pltpu.CompilerParams(
            collective_id=0, has_side_effects=True, vmem_limit_bytes=56 * MIB
        ),
        cost_estimate=pl.CostEstimate(
            flops=2 * n * n * nf, bytes_accessed=4 * n * nf, transcendentals=0
        ),
        name="exchange",
    )(statistic, gradient)
    pre, next_m, diag = pl.pallas_call(
        functools.partial(newton_kernel, R, C),
        out_shape=(
            jax.ShapeDtypeStruct((n, nf), BF16),
            jax.ShapeDtypeStruct((bs, width), F32),
            jax.ShapeDtypeStruct((bs, 1), F32),
        ),
        in_specs=[hbm, vmem, vmem, vmem],
        out_specs=(hbm, vmem, vmem),
        scratch_shapes=[
            pltpu.VMEM((2, bs, n), F32),
            pltpu.VMEM((2, bs, n), BF16),
            dma((R,)),
        ],
        compiler_params=pltpu.CompilerParams(vmem_limit_bytes=48 * MIB),
        cost_estimate=pl.CostEstimate(
            flops=8 * bs * n * n, bytes_accessed=4 * n * nf, transcendentals=0
        ),
        name="newton",
    )(y, sf, statistic, info)
    return next_m, pre, diag.reshape(bs)


def local_plain(statistic, gradient):
    n = gradient.shape[0]
    rows_here, cols_here = statistic.shape
    total = lax.psum(jnp.sum(statistic * statistic), ("row", "col"))
    scale4, root = coefficients(total, n)
    row_ids = lax.axis_index("row") * rows_here + jnp.arange(rows_here, dtype=jnp.int32)
    col_start = lax.axis_index("col") * cols_here
    col_ids = col_start + jnp.arange(cols_here, dtype=jnp.int32)
    own = row_ids[:, None] == col_ids[None, :]
    left = jnp.where(own, statistic - statistic.astype(BF16).astype(F32), 0.0)
    low_here = lax.dynamic_update_slice(
        jnp.zeros((n,), F32), jnp.sum(left, axis=0), (col_start,)
    )
    low = lax.psum(low_here, ("row", "col"))
    wide = lax.all_gather(statistic.astype(BF16), "col", axis=1, tiled=True)
    whole = lax.all_gather(wide, "row", axis=0, tiled=True)
    prod = jnp.dot(whole, gradient, preferred_element_type=F32)
    pre = ((1.25 * gradient.astype(F32) - prod * (0.25 / scale4)) / root).astype(BF16)
    every = jnp.arange(n, dtype=jnp.int32)
    ident = row_ids[:, None] == every[None, :]
    r = (wide.astype(F32) + jnp.where(ident, low[None, :], 0.0)) / scale4
    for _ in range(4):
        prod = jnp.dot(r.astype(BF16), whole, preferred_element_type=F32)
        r = 1.25 * r - 0.25 * (prod + r * low[None, :]) / scale4
    next_diag = jnp.sum(jnp.where(ident, r, 0.0), axis=1)
    next_m = jnp.where(own, 0.0, lax.dynamic_slice_in_dim(r, col_start, cols_here, 1))
    return next_m, pre, next_diag


def solution(mesh):
    R, C = mesh.shape["row"], mesh.shape["col"]
    local = functools.partial(local_kernels, R, C) if C == 2 and R % C == 0 else local_plain
    return jax.shard_map(
        local,
        mesh=mesh,
        in_specs=(P(("section", "row"), "col"), P("section", ("row", "col"))),
        out_specs=(
            P(("section", "row"), "col"),
            P("section", ("row", "col")),
            P(("section", "row")),
        ),
        check_vma=False,
    )
```

time: 489 us -> 534 us (1.092)
  Pallas kernels: 0 us -> 532 us
  waiting for transfers between devices: 293 us -> 0 us
  matrix products: 137 us -> 0 us
  blocking collectives: 21.7 us -> 0 us
  local copies, waits for them, and re-layouts: 14.8 us -> 0.7 us
  between operations: 14.6 us -> 0.67 us
  other arithmetic: 7.21 us -> 0.73 us
    pallas_call x0 -> x2, Pallas kernels: none -> 532 us  [the longest x1 451 us: local_kernels(): pl.pallas_call(functools.partial(newton_kernel, R, C), out_shape=(jax.Sha...]
    all_gather x5 -> x0, waiting for transfers between devices: 292 us -> none  [the longest x1 153 us: local(): m_cols = lax.all_gather(m_start, 'row', axis=0, tiled=True)]
    dot_general x4 -> x0, matrix products: 137 us -> none  [the longest x1 82.3 us: local(): jnp.einsum('aijc,jcf->iaf', arranged, grad_split, preferred_element_type=...]
    psum x2 -> x0, blocking collectives: 21.7 us -> none  [the longest x1 18.7 us: local(): total = lax.psum(jnp.sum(statistic * statistic), ('row', 'col'))]
    reshape x1 -> x0, local copies, waits for them, and re-layouts: 14.8 us -> none  [local(): arranged = spread.reshape(rows_here, grid_rows, grid_cols, cols_here)]
  transfers between devices with their start and end apart: 5 -> 0, of which waited for: 5 -> 0; matrix products, arithmetic and copies ran while one was open for 24% -> 0% of each run, Pallas kernels for 0% -> 0%
where the time goes in v1:
time: 534 us
  Pallas kernels  532 us (100%)
    pallas_call x1, Pallas kernels, local_kernels(): pl.pallas_call(functools.partial(newton_kernel, R, C), out_shape=(jax.Sha...  451 us
    pallas_call x1, Pallas kernels, local_kernels(): pl.pallas_call(functools.partial(exchange_kernel, R, C), out_shape=(jax.S...  81.4 us

profile of v1, /device:TPU:0, one launch (start us, length us, event | category | flops | bytes accessed | tf_op | source)
XLA Modules:
  0.0 534.0 jit_solution(1445191678270693597)
XLA Ops:
  0.6 0.0 copy-start
  0.6 81.4 %exchange.1 = (bf16[2048,3584]{1,0:T(8,128)(2,1)}, bf16[2048,2048]{1,0:T(8,128)(2,1)}, f32[1,2176]{1,0:T(1,128)}) custom-call(f32[512,1024]{1,0:T(8,128)} %s_ref.3, bf16[2048,3584]{1,0:T(8,128)(2,1)} %g_ref.1), custom_call_target="tpu_custom_call" | custom-call | flops 30064771072 | bytes 29360128 | tf_op jit(solution)/shard_map/exchange/pallas_call | solution.py:319
  82.1 0.0 copy-done
  82.1 0.0 copy-start.1
  82.1 0.7 copy-done.1
  82.8 450.5 %newton.1 = (bf16[2048,3584]{1,0:T(8,128)(2,1)}, f32[512,1024]{1,0:T(8,128)}, f32[512,1]{1,0:T(8,128)S(1)}) custom-call(bf16[2048,3584]{1,0:T(8,128)(2,1)} %get-tuple-element.9.y_ref, bf16[2048,2048]{1,0:T(8,128)(2,1)} %get-tuple-element.10.sf, f32[512,1024]{1,0:T(8,128)S(1)} %copy-done, f32[1,2176]{1,0:T(1,128)S(1)} %copy-done.1), custom_call_target="tpu_custom_call" | custom-call | flops 17179869184 | bytes 29360128 | tf_op jit(solution)/shard_map/newton/pallas_call | solution.py:346
  533.3 0.7 reduce
Async XLA Ops:
  0.6 81.4 %copy-start = (f32[512,1024]{1,0:T(8,128)S(1)}, f32[512,1024]{1,0:T(8,128)}, u32[]{:S(2)}) copy-start(f32[512,1024]{1,0:T(8,128)} %s_ref.3) | copy-start | bytes 6291460
  82.1 0.7 copy-start.1

commit v2 on v1

--- a/solution.py
+++ b/solution.py
@@ -235,18 +235,22 @@
 
 def newton_kernel(
     R, C, y_ref, sf, s_ref, info_ref, pre_ref, next_ref, diag_ref,
-    held, narrow, y_sem,
+    held, narrow, yv, in_sem, out_sem,
 ):
     z, c = lax.axis_index("row"), lax.axis_index("col")
     bs, width = s_ref.shape
     n = sf.shape[0]
 
-    def y_copy(i):
+    def y_in(i):
         rows = pl.ds(i * bs, bs)
-        return pltpu.make_async_copy(y_ref.at[rows], pre_ref.at[rows], y_sem.at[i])
+        return pltpu.make_async_copy(y_ref.at[rows], yv.at[rows], in_sem.at[i])
+
+    def y_out(i):
+        rows = pl.ds(i * bs, bs)
+        return pltpu.make_async_copy(yv.at[rows], pre_ref.at[rows], out_sem.at[i])
 
     for i in range(R):
-        y_copy(i).start()
+        y_in(i).start()
 
     scale4, _ = coefficients(info_ref[:, pl.ds(n, 1)], n)
     inv = 1.0 / scale4
@@ -285,7 +289,11 @@
             return inner
         lax.fori_loop(0, n // chunk, body, 0)
         return carry
-    lax.fori_loop(0, 3, turn, 0)
+    turn(0, 0)
+    for i in range(R):
+        y_in(i).wait()
+        y_out(i).start()
+    lax.fori_loop(1, 3, turn, 0)
 
     def last(j, carry):
         at = pl.multiple_of(c * width + j * chunk, chunk)
@@ -307,7 +315,7 @@
     diag_ref[...] = lax.fori_loop(0, n // chunk, diagonal, jnp.zeros((bs, 1), F32))
 
     for i in range(R):
-        y_copy(i).wait()
+        y_out(i).wait()
 
 
 def local_kernels(R, C, statistic, gradient):
@@ -355,9 +363,10 @@
         scratch_shapes=[
             pltpu.VMEM((2, bs, n), F32),
             pltpu.VMEM((2, bs, n), BF16),
-            dma((R,)),
+            pltpu.VMEM((n, nf), BF16),
+            dma((R,)), dma((R,)),
         ],
-        compiler_params=pltpu.CompilerParams(vmem_limit_bytes=48 * MIB),
+        compiler_params=pltpu.CompilerParams(vmem_limit_bytes=56 * MIB),
         cost_estimate=pl.CostEstimate(
             flops=8 * bs * n * n, bytes_accessed=4 * n * nf, transcendentals=0
         ),

time: 534 us -> 111 us (0.21)
  Pallas kernels: 532 us -> 109 us
    pallas_call x1, Pallas kernels: 451 us -> 27.6 us  [local_kernels(): pl.pallas_call(functools.partial(newton_kernel, R, C), out_shape=(jax.Sha...]
where the time goes in v2:
time: 111 us
  Pallas kernels  109 us (98%)
  other arithmetic  1.68 us (2%)
    pallas_call x1, Pallas kernels, local_kernels(): pl.pallas_call(functools.partial(exchange_kernel, R, C), out_shape=(jax.S...  81.3 us
    pallas_call x1, Pallas kernels, local_kernels(): pl.pallas_call(functools.partial(newton_kernel, R, C), out_shape=(jax.Sha...  27.6 us

profile of v2, /device:TPU:0, one launch (start us, length us, event | category | flops | bytes accessed | tf_op | source)
XLA Modules:
  0.0 111.2 jit_solution(11070646575720924875)
XLA Ops:
  0.6 81.3 %exchange.1 = (bf16[2048,3584]{1,0:T(8,128)(2,1)}, bf16[2048,2048]{1,0:T(8,128)(2,1)}, f32[1,2176]{1,0:T(1,128)}) custom-call(f32[512,1024]{1,0:T(8,128)} %s_ref.3, bf16[2048,3584]{1,0:T(8,128)(2,1)} %g_ref.1), custom_call_target="tpu_custom_call" | custom-call | flops 30064771072 | bytes 29360128 | tf_op jit(solution)/shard_map/exchange/pallas_call | solution.py:327
  81.9 27.6 %newton.1 = (bf16[2048,3584]{1,0:T(8,128)(2,1)}, f32[512,1024]{1,0:T(8,128)}, f32[512,1]{1,0:T(8,128)}) custom-call(bf16[2048,3584]{1,0:T(8,128)(2,1)} %get-tuple-element.9.y_ref, bf16[2048,2048]{1,0:T(8,128)(2,1)} %get-tuple-element.10.sf, f32[512,1024]{1,0:T(8,128)} %s_ref.3, f32[1,2176]{1,0:T(1,128)} %get-tuple-element.11.info_ref), custom_call_target="tpu_custom_call" | custom-call | flops 17179869184 | bytes 29360128 | tf_op jit(solution)/shard_map/newton/pallas_call | solution.py:354
  109.5 1.7 %reduce = f32[512]{0:T(512)} reduce(f32[512,1]{1,0:T(8,128)} %get-tuple-element.14, f32[]{:T(128)} %constant), dimensions={1}, to_apply=%get-tuple-element.14.reduce_sub_computation | reduce | bytes 4100 | tf_op jit(solution)/shard_map/newton/pallas_call | solution.py:354
